TPU v7x, 256 devices: a whole 4x4x8 slice. The times are simulated.
256 devices in a mesh: tile: 64 (over y, z, core), panel: 4 (over x).
Axes of the slice: x: 4, y: 4, z: 8, core: 2. Of those that a mesh axis runs over, the one named last changes fastest.
Arguments:
- wavefield: bfloat16 [2, 16384, 64], P(None, ('tile', 'panel')), may hold values from -6 to 6
- residual: bfloat16 [2, 16384, 64], P(None, ('tile', 'panel')), may hold values from -6 to 6
- v_factors: bfloat16 [64, 64, 2, 256, 128], P(None, 'tile', None, 'panel'), may hold values from -0.375 to 0.375
- u_factors: bfloat16 [64, 64, 2, 256, 128], P('tile', None, None, 'panel'), may hold values from -0.09375 to 0.09375
- tile_ranks: int32 [64, 64], replicated, may hold values from 1 to 128
- tile_present: int32 [64, 64], replicated, may hold values 0 or 1
Outputs:
- predicted: bfloat16 [2, 16384, 64], P(None, ('tile', 'panel'))
- gradient: bfloat16 [2, 16384, 64], P(None, ('tile', 'panel'))
All inputs are finite; a program needn't handle non-finite values.
Results may differ from a plain program's by a relative error of at most 0.018.
Values may be sent and summed in bfloat16 or wider, within the bound.
A program may use at most 64 MiB of HBM per device.

v0:
```python
import jax
import jax.numpy as jnp
from jax import lax
from jax.sharding import PartitionSpec as P


def conj_product(factor, vector, weight):
    sources = vector.shape[2]
    joined = jnp.concatenate([vector[0], vector[1]], axis=1)
    first = jnp.einsum("nrk,rs->nsk", factor[:, 0], joined, preferred_element_type=jnp.float32)
    second = jnp.einsum("nrk,rs->nsk", factor[:, 1], joined, preferred_element_type=jnp.float32)
    real_part = first[:, :sources] + second[:, sources:]
    imag_part = first[:, sources:] - second[:, :sources]
    parts = jnp.stack([real_part, imag_part], axis=1)
    return parts * weight[:, None, None, :]


def out_product(factor, space):
    first = jnp.einsum("nrk,ncsk->crs", factor[:, 0], space, preferred_element_type=jnp.float32)
    second = jnp.einsum("nrk,ncsk->crs", factor[:, 1], space, preferred_element_type=jnp.float32)
    real_part = first[0] - second[1]
    imag_part = first[1] + second[0]
    return jnp.stack([real_part, imag_part], axis=0).astype(jnp.bfloat16)


def regroup(partial_value):
    moved = lax.all_to_all(
        partial_value.astype(jnp.bfloat16), "tile", split_axis=0, concat_axis=0, tiled=True
    )
    total = lax.psum(moved.astype(jnp.float32).astype(jnp.bfloat16), "panel")
    return total


def weights(rank_row, present_row, levels):
    keep = (jnp.arange(levels, dtype=jnp.int32)[None, :] < rank_row[:, None]) & (
        present_row[:, None] == 1
    )
    return keep.astype(jnp.float32)


def on_device(wavefield, residual, v_factors, u_factors, tile_ranks, tile_present):
    levels = v_factors.shape[4]
    owner = lax.axis_index("tile")
    v_local = v_factors[:, 0]
    u_local = u_factors[0]
    col_ranks = lax.dynamic_slice_in_dim(tile_ranks, owner, 1, 1)[:, 0]
    col_present = lax.dynamic_slice_in_dim(tile_present, owner, 1, 1)[:, 0]
    row_ranks = lax.dynamic_slice_in_dim(tile_ranks, owner, 1, 0)[0]
    row_present = lax.dynamic_slice_in_dim(tile_present, owner, 1, 0)[0]
    col_weight = weights(col_ranks, col_present, levels)
    row_weight = weights(row_ranks, row_present, levels)
    fspace = regroup(conj_product(v_local, wavefield, col_weight))
    predicted = out_product(u_local, fspace)
    aspace = regroup(conj_product(u_local, residual, row_weight))
    gradient = out_product(v_local, aspace)
    return (predicted, gradient)


def solution(mesh):
    return jax.shard_map(
        on_device,
        mesh=mesh,
        in_specs=(
            P(None, ("tile", "panel"), None),
            P(None, ("tile", "panel"), None),
            P(None, "tile", None, "panel", None),
            P("tile", None, None, "panel", None),
            P(),
            P(),
        ),
        out_specs=(P(None, ("tile", "panel"), None), P(None, ("tile", "panel"), None)),
        check_vma=False,
    )
```

profile of v0, /device:TPU:1, one launch (start us, length us, event | category | flops | bytes accessed | tf_op | source)
XLA Modules:
  0.0 256.1 jit_solution(1922389218061086821)
XLA Ops:
  7.2 0.0 copy-start
  7.2 0.0 copy-start.3
  7.2 1.8 copy.31
  9.0 0.0 copy-done.3
  9.0 2.8 %convolution_bitcast_fusion.2 = f32[64,128,128]{2,1,0:T(8,128)} fusion(bf16[64,2,64,128]{3,2,0,1:T(8,128)(2,1)S(1)} %bitcast.90, bf16[64,64]{1,0:T(8,128)(2,1)S(1)} %get-tuple-element.21, bf16[64,64]{1,0:T(8,128)(2,1)S(1)} %get-tuple-element.20), kind=kOutput, calls=%fused_computation.6 | convolution fusion | flops 134250496 | bytes 5275648 | tf_op jit(solution)/shard_map/nrk,rs->nsk/dot_general | solution.py:11
  11.8 0.0 copy-start.4
  11.8 2.8 %convolution_bitcast_fusion.3 = f32[64,128,128]{2,1,0:T(8,128)} fusion(bf16[64,2,64,128]{3,2,0,1:T(8,128)(2,1)S(1)} %bitcast.91, bf16[64,64]{1,0:T(8,128)(2,1)S(1)} %get-tuple-element.21, bf16[64,64]{1,0:T(8,128)(2,1)S(1)} %get-tuple-element.20), kind=kOutput, calls=%fused_computation.7 | convolution fusion | flops 134250496 | bytes 5275648 | tf_op jit(solution)/shard_map/nrk,rs->nsk/dot_general | solution.py:10
  14.6 0.0 copy-done
  14.6 0.2 dynamic-slice_reduce_fusion
  14.7 0.0 copy-done.4
  14.8 0.2 fusion.28
  14.9 4.4 %fusion.5 = (f32[64,1,64,128]{3,2,0,1:T(8,128)S(1)}, f32[64,1,64,128]{3,2,0,1:T(8,128)S(1)}) fusion(f32[64,128,128]{2,1,0:T(8,128)} %convolution_bitcast_fusion.2, f32[64,128,128]{2,1,0:T(8,128)} %convolution_bitcast_fusion.3), kind=kLoop, calls=%fused_computation.15 | loop fusion | flops 1048576 | bytes 12582912 | tf_op jit(solution)/shard_map/stack | solution.py:14
  19.4 0.1 fusion.27
  19.5 0.7 fusion
  20.1 1.6 copy.17
  21.7 13.3 %all-to-all-start = ((bf16[64,2,64,128]{3,2,1,0:T(8,128)(2,1)}), bf16[64,2,64,128]{3,2,1,0:T(8,128)(2,1)}, u32[]{:S(2)}, u32[]{:S(2)}) async-start(bf16[64,2,64,128]{3,2,1,0:T(8,128)(2,1)} %copy.17), calls=%async_computation | async-start | bytes 4194304 | tf_op jit(solution)/shard_map/all_to_all | solution.py:27
  35.0 0.0 copy-start.5
  35.0 1.8 copy.30
  36.8 0.0 copy-start.1
  36.9 0.1 fusion.30
  37.0 0.0 copy-done.5
  37.0 0.8 convolution_bitcast_fusion
  37.8 0.3 copy-done.1
  38.1 0.8 convolution_bitcast_fusion.1
  38.9 1.4 fusion.3
  40.3 0.6 fusion.1
  41.0 1.6 copy.20
  42.6 43.6 %all-to-all-done = bf16[64,2,64,128]{3,2,1,0:T(8,128)(2,1)} async-done(((bf16[64,2,64,128]{3,2,1,0:T(8,128)(2,1)}), bf16[64,2,64,128]{3,2,1,0:T(8,128)(2,1)}, u32[]{:S(2)}, u32[]{:S(2)}) %all-to-all-start) | async-done | bytes 2097184 | tf_op jit(solution)/shard_map/all_to_all | solution.py:27
  86.2 6.0 %all-to-all-start.1 = ((bf16[64,2,64,128]{3,2,1,0:T(8,128)(2,1)}), bf16[64,2,64,128]{3,2,1,0:T(8,128)(2,1)}, u32[]{:S(2)}, u32[]{:S(2)}) async-start(bf16[64,2,64,128]{3,2,1,0:T(8,128)(2,1)} %copy.20), calls=%async_computation.1 | async-start | bytes 4194304 | tf_op jit(solution)/shard_map/all_to_all | solution.py:27
  92.2 0.0 all-reduce.3.cloned.1.call-start
  92.3 3.1 %copy.18 = bf16[64,2,64,128]{3,2,0,1:T(8,128)(2,1)} copy(bf16[64,2,64,128]{3,2,1,0:T(8,128)(2,1)} %all-to-all-done) | data formatting | bytes 4194304 | tf_op jit(solution)/shard_map/all_to_all | solution.py:27
  95.4 48.0 %all-to-all-done.1 = bf16[64,2,64,128]{3,2,1,0:T(8,128)(2,1)} async-done(((bf16[64,2,64,128]{3,2,1,0:T(8,128)(2,1)}), bf16[64,2,64,128]{3,2,1,0:T(8,128)(2,1)}, u32[]{:S(2)}, u32[]{:S(2)}) %all-to-all-start.1) | async-done | bytes 2097184 | tf_op jit(solution)/shard_map/all_to_all | solution.py:27
  143.4 3.2 %copy.21 = bf16[64,2,64,128]{3,2,0,1:T(8,128)(2,1)} copy(bf16[64,2,64,128]{3,2,1,0:T(8,128)(2,1)} %all-to-all-done.1) | data formatting | bytes 4194304 | tf_op jit(solution)/shard_map/all_to_all | solution.py:27
  146.5 0.0 all-reduce.3.cloned.1.call-update
  146.5 94.7 %all-reduce.3.cloned.1.call-done = (bf16[64,2,64,128]{3,2,0,1:T(8,128)(2,1)}, bf16[64,2,64,128]{3,2,0,1:T(8,128)(2,1)}) async-done(((bf16[64,2,64,128]{3,2,0,1:T(8,128)(2,1)}, bf16[64,2,64,128]{3,2,0,1:T(8,128)(2,1)}), (bf16[64,2,64,128]{3,2,0,1:T(8,128)(2,1)}, bf16[64,2,64,128]{3,2,0,1:T(8,128)(2,1)})) %all-reduce.3.cloned.1.call-update) | async-done | bytes 4194320 | tf_op jit(solution)/shard_map/psum | solution.py:30
  241.2 0.0 copy-start.2
  241.2 2.7 %convolution_bitcast_fusion.6 = f32[2,64,64]{1,2,0:T(8,128)S(1)} fusion(bf16[64,2,64,128]{3,2,0,1:T(8,128)(2,1)} %get-tuple-element.8, bf16[64,2,64,128]{3,2,0,1:T(8,128)(2,1)} %bitcast.96), kind=kOutput, calls=%fused_computation.20 | convolution fusion | flops 134217728 | bytes 3178496 | tf_op jit(solution)/shard_map/nrk,ncsk->crs/dot_general | solution.py:20
  243.9 0.0 copy-done.2
  243.9 0.0 copy-start.6
  243.9 2.4 convolution_bitcast_fusion.7
  246.4 0.0 copy-done.6
  246.4 0.7 convolution_bitcast_fusion.4
  247.1 0.7 convolution_bitcast_fusion.5
  247.8 0.7 copy.22
  248.5 0.7 copy.23
  (8 shorter events, 0.1 us)
Async XLA Ops:
  7.2 7.4 %copy-start = (s32[64,64]{1,0:T(8,128)S(1)}, s32[64,64]{1,0:T(8,128)}, u32[]{:S(2)}) copy-start(s32[64,64]{1,0:T(8,128)} %param.10) | copy-start | bytes 49156
  7.2 1.8 copy-start.3
  11.8 3.0 %copy-start.4 = (s32[64,64]{1,0:T(8,128)S(1)}, s32[64,64]{1,0:T(8,128)}, u32[]{:S(2)}) copy-start(s32[64,64]{1,0:T(8,128)} %param.11) | copy-start | bytes 49156
  21.7 64.5 %all-to-all-start = ((bf16[64,2,64,128]{3,2,1,0:T(8,128)(2,1)}), bf16[64,2,64,128]{3,2,1,0:T(8,128)(2,1)}, u32[]{:S(2)}, u32[]{:S(2)}) async-start(bf16[64,2,64,128]{3,2,1,0:T(8,128)(2,1)} %copy.17), calls=%async_computation | async-start | bytes 4194304 | tf_op jit(solution)/shard_map/all_to_all | solution.py:27
  35.0 1.9 copy-start.5
  36.8 1.3 copy-start.1
  86.2 57.2 %all-to-all-start.1 = ((bf16[64,2,64,128]{3,2,1,0:T(8,128)(2,1)}), bf16[64,2,64,128]{3,2,1,0:T(8,128)(2,1)}, u32[]{:S(2)}, u32[]{:S(2)}) async-start(bf16[64,2,64,128]{3,2,1,0:T(8,128)(2,1)} %copy.20), calls=%async_computation.1 | async-start | bytes 4194304 | tf_op jit(solution)/shard_map/all_to_all | solution.py:27
  92.2 149.0 %all-reduce.3.cloned.1.call-start = ((), (), s32[]{:S(2)}) async-start(), calls=%async_computation.2 | async-start | bytes 8388608 | tf_op jit(solution)/shard_map/psum | solution.py:30
  241.2 2.7 %copy-start.2 = (bf16[1,64,2,64,128]{4,3,1,2,0:T(8,128)(2,1)S(1)}, bf16[1,64,2,64,128]{4,3,1,2,0:T(8,128)(2,1)}, u32[]{:S(2)}) copy-start(bf16[1,64,2,64,128]{4,3,1,2,0:T(8,128)(2,1)} %copy-done.1) | copy-start | bytes 6291460
  243.9 2.4 copy-start.6
Sparse Core Ops, SparseCore 0:
  146.7 94.5 all-reduce.2
where the time goes:
time: 257 us; the launch traced here: 256 us
  waiting for transfers between devices  186 us (72%)
  starting transfers between devices  19.4 us (8%)
  local copies, waits for them, and re-layouts  15 us (6%)
  between operations  14.3 us (6%)
  matrix products  13.6 us (5%)
  other arithmetic  7.49 us (3%)
    psum x1, waiting for transfers between devices, regroup(): total = lax.psum(moved.astype(jnp.float32).astype(jnp.bfloat16), 'panel')  94.7 us
    all_to_all x2, waiting for transfers between devices, regroup(): lax.all_to_all(partial_value.astype(jnp.bfloat16), 'tile', split_axis=0,...  91.6 us
    all_to_all x2, starting transfers between devices, regroup(): lax.all_to_all(partial_value.astype(jnp.bfloat16), 'tile', split_axis=0,...  19.3 us
    all_to_all x2, local copies, waits for them, and re-layouts, regroup(): lax.all_to_all(partial_value.astype(jnp.bfloat16), 'tile', split_axis=0,...  6.26 us
    another operation x2, other arithmetic, conj_product(): parts = jnp.stack([real_part, imag_part], axis=1)  5.79 us
    unnamed x18, local copies, waits for them, and re-layouts  5.37 us
  transfers between devices with their start and end apart: 3, of which 3 were waited for; matrix products, arithmetic and copies ran while one was open for 4% of the time, Pallas kernels for 0%

commit v1 on v0

v1 whole, which is shorter than its diff:
```python
import functools

import jax
import jax.numpy as jnp
from jax import lax
from jax.experimental import pallas as pl
from jax.experimental.pallas import tpu as pltpu
from jax.sharding import PartitionSpec as P

MESH = pl.DeviceIdType.MESH
PANELS = 4
V_CHUNKS = (4, 4, 4, 4)
U_CHUNKS = (4, 4, 4, 2, 1, 1)


def spans(sizes):
    starts = []
    at = 0
    for size in sizes:
        starts.append((at, size))
        at += size
    return starts


def kernel(
    groups,
    wave_hbm, resid_hbm, v_hbm, u_hbm, rank_hbm, present_hbm,
    pred_ref, grad_ref,
    raw, joined, vec_w, vec_r, v_all, u_all, f_send, f_recv, a_send, a_recv,
    acc_p, acc_g, own_sum, part_send, part_recv, ranks, present,
    raw_sem, rank_sem, own_sem, x_send, x_recv, v_ssem, v_rsem, u_ssem, u_rsem,
    f_ssem, f_rsem, a_ssem, a_rsem, p_ssem, p_rsem,
):
    t = lax.axis_index("tile")
    p = lax.axis_index("panel")
    me = t // PANELS
    low = t % PANELS
    q = (p + PANELS - low) % PANELS
    alone = q == low

    raw_copies = [
        pltpu.make_async_copy(wave_hbm, raw.at[0], raw_sem.at[0]),
        pltpu.make_async_copy(resid_hbm, raw.at[1], raw_sem.at[1]),
    ]
    rank_copies = [
        pltpu.make_async_copy(rank_hbm, ranks, rank_sem.at[0]),
        pltpu.make_async_copy(present_hbm, present, rank_sem.at[1]),
    ]
    own_copies = [
        pltpu.make_async_copy(v_hbm.at[:, q], v_all.at[:, :, p], own_sem.at[0]),
        pltpu.make_async_copy(u_hbm.at[:, q], u_all.at[:, :, p], own_sem.at[1]),
    ]
    for copy in raw_copies + rank_copies:
        copy.start()

    barrier = pltpu.get_barrier_semaphore()
    for d in (1, 2, 3):
        pl.semaphore_signal(barrier, inc=1, device_id=(t, (p + d) % PANELS), device_id_type=MESH)

    def greet(n, carry):
        other = PANELS * n + q

        @pl.when(other != t)
        def _():
            pl.semaphore_signal(barrier, inc=1, device_id=(other, p), device_id_type=MESH)

        return carry

    lax.fori_loop(0, groups, greet, 0)
    for copy in own_copies:
        copy.start()
    for copy in raw_copies:
        copy.wait()
    for k in (0, 1):
        joined[k, p] = jnp.concatenate([raw[k, 0], raw[k, 1]], axis=1)

    @pl.when(alone)
    def _():
        pl.semaphore_wait(barrier, 3 + groups - 1)

    @pl.when(jnp.logical_not(alone))
    def _():
        pl.semaphore_wait(barrier, 3 + groups)

    def vec_copy(d):
        return pltpu.make_async_remote_copy(
            joined.at[:, p], joined.at[:, p], x_send.at[d - 1], x_recv.at[d - 1],
            device_id=(t, (p + d) % PANELS), device_id_type=MESH,
        )

    def vec_arrival(d):
        source = (p + PANELS - d) % PANELS
        return pltpu.make_async_remote_copy(
            joined.at[:, source], joined.at[:, source], x_send.at[d - 1], x_recv.at[d - 1],
            device_id=(t, source), device_id_type=MESH,
        )

    def factor_copy(src, dst, ssem, rsem, c, start, size, d):
        return pltpu.make_async_remote_copy(
            src.at[pl.ds(start, size), (q + d) % PANELS],
            dst.at[pl.ds(start, size), :, p],
            ssem.at[c, d - 1], rsem.at[c, d - 1],
            device_id=(t, (p + d) % PANELS), device_id_type=MESH,
        )

    def factor_arrival(src, dst, ssem, rsem, c, start, size, d):
        source = (p + PANELS - d) % PANELS
        return pltpu.make_async_remote_copy(
            src.at[pl.ds(start, size), q],
            dst.at[pl.ds(start, size), :, source],
            ssem.at[c, d - 1], rsem.at[c, d - 1],
            device_id=(t, source), device_id_type=MESH,
        )

    for d in (1, 3, 2):
        vec_copy(d).start()
    v_spans = spans(V_CHUNKS)
    u_spans = spans(U_CHUNKS)
    for c, (start, size) in enumerate(v_spans):
        for d in (2, 1, 3):
            factor_copy(v_hbm, v_all, v_ssem, v_rsem, c, start, size, d).start()
    for c, (start, size) in enumerate(u_spans):
        for d in (2, 1, 3):
            factor_copy(u_hbm, u_all, u_ssem, u_rsem, c, start, size, d).start()

    acc_p[...] = jnp.zeros_like(acc_p)
    acc_g[...] = jnp.zeros_like(acc_g)
    for copy in rank_copies:
        copy.wait()
    for d in (1, 3, 2):
        vec_arrival(d).wait_recv()
    for k, vec in ((0, vec_w), (1, vec_r)):
        rows = joined[k].reshape(256, 128).astype(jnp.float32).T
        vec[:, :256] = rows.astype(jnp.bfloat16)
        vec[:, 256:] = jnp.concatenate([rows[64:], -rows[:64]], axis=0).astype(jnp.bfloat16)

    def block_copy(send, recv, ssem, rsem, n):
        return pltpu.make_async_remote_copy(
            send.at[n], recv.at[me], ssem.at[n], rsem.at[me],
            device_id=(PANELS * n + q, p), device_id_type=MESH,
        )

    def block_own(send, recv, rsem, n):
        return pltpu.make_async_copy(send.at[n], recv.at[n], rsem.at[n])

    levels = lax.broadcasted_iota(jnp.int32, (1, 128), 1)

    def project(factor, vec, send, recv, ssem, rsem, start, size, column):
        for n0 in range(start, start + size, 2):
            many = min(2, start + size - n0)
            joint = [factor[n0 + k].reshape(512, 128) for k in range(many)]
            joint = joint[0] if many == 1 else jnp.concatenate(joint, axis=1)
            space = jnp.dot(vec[...], joint, preferred_element_type=jnp.float32)
            for k in range(many):
                n = n0 + k
                other = PANELS * n + q
                if column:
                    rank, here = ranks[other, t], present[other, t]
                else:
                    rank, here = ranks[t, other], present[t, other]
                limit = jnp.where(here == 1, rank, 0)
                part = jnp.where(levels < limit, space[:, 128 * k : 128 * (k + 1)], 0.0)
                send[n] = part.astype(jnp.bfloat16)

                @pl.when(other != t)
                def _():
                    block_copy(send, recv, ssem, rsem, n).start()

                @pl.when(other == t)
                def _():
                    block_own(send, recv, rsem, n).start()

    def expand(factor, recv, rsem, acc, start, size):
        for n0 in range(start, start + size, 2):
            many = min(2, start + size - n0)
            for k in range(many):
                block_own(recv, recv, rsem, n0 + k).wait()
            left = [factor[n0 + k].reshape(512, 128) for k in range(many)]
            right = [recv[n0 + k] for k in range(many)]
            left = left[0] if many == 1 else jnp.concatenate(left, axis=1)
            right = right[0] if many == 1 else jnp.concatenate(right, axis=1)
            acc[...] += lax.dot_general(
                left, right, (((1,), (1,)), ((), ())), preferred_element_type=jnp.float32
            )

    def part_copy(k, d):
        target = (p + d) % PANELS
        return pltpu.make_async_remote_copy(
            part_send.at[k, target], part_recv.at[k, d - 1], p_ssem.at[k, d - 1], p_rsem.at[k, d - 1],
            device_id=(t, target), device_id_type=MESH,
        )

    def send_parts(k, acc):
        lanes = lax.broadcasted_iota(jnp.int32, (256, 128), 1)
        turned = pltpu.roll(acc[256:, :], 64, 1)
        total = acc[:256, :] + jnp.where(lanes < 64, -turned, turned)
        total = total.reshape(PANELS, 64, 128)
        own_sum[k] = total
        part_send[k] = total.astype(jnp.bfloat16)
        for d in (2, 1, 3):
            part_copy(k, d).start()

    def finish(k, out):
        for d in (1, 3, 2):
            part_copy(k, d).wait_recv()
        total = own_sum[k, p]
        for d in (1, 2, 3):
            total = total + part_recv[k, d - 1].astype(jnp.float32)
        out[0] = total[:, :64].astype(jnp.bfloat16)
        out[1] = total[:, 64:].astype(jnp.bfloat16)

    own_copies[0].wait()
    for c, (start, size) in enumerate(v_spans):
        for d in (1, 3, 2):
            factor_arrival(v_hbm, v_all, v_ssem, v_rsem, c, start, size, d).wait_recv()
        project(v_all, vec_w, f_send, f_recv, f_ssem, f_rsem, start, size, True)
    own_copies[1].wait()
    for c, (start, size) in enumerate(u_spans):
        for d in (1, 3, 2):
            factor_arrival(u_hbm, u_all, u_ssem, u_rsem, c, start, size, d).wait_recv()
        project(u_all, vec_r, a_send, a_recv, a_ssem, a_rsem, start, size, False)
        expand(u_all, f_recv, f_rsem, acc_p, start, size)
        if c > 0:
            expand(v_all, a_recv, a_rsem, acc_g, *u_spans[c - 1])
    send_parts(0, acc_p)
    expand(v_all, a_recv, a_rsem, acc_g, *u_spans[-1])
    send_parts(1, acc_g)
    finish(0, pred_ref)
    finish(1, grad_ref)

    for d in (1, 2, 3):
        vec_copy(d).wait_send()
        for c, (start, size) in enumerate(v_spans):
            factor_copy(v_hbm, v_all, v_ssem, v_rsem, c, start, size, d).wait_send()
        for c, (start, size) in enumerate(u_spans):
            factor_copy(u_hbm, u_all, u_ssem, u_rsem, c, start, size, d).wait_send()
        for k in (0, 1):
            part_copy(k, d).wait_send()

    def settle(n, carry):
        @pl.when(PANELS * n + q != t)
        def _():
            block_copy(f_send, f_recv, f_ssem, f_rsem, n).wait_send()
            block_copy(a_send, a_recv, a_ssem, a_rsem, n).wait_send()

        return carry

    lax.fori_loop(0, groups, settle, 0)


def on_device(wavefield, residual, v_factors, u_factors, tile_ranks, tile_present):
    tiles = tile_ranks.shape[0]
    groups = tiles // PANELS
    v_local = v_factors.reshape(groups, PANELS, 2, 64, 128)
    u_local = u_factors.reshape(groups, PANELS, 2, 64, 128)
    hbm = pl.BlockSpec(memory_space=pl.ANY)
    vmem = pl.BlockSpec(memory_space=pltpu.VMEM)
    b16, f32 = jnp.bfloat16, jnp.float32
    dma = pltpu.SemaphoreType.DMA
    result = jax.ShapeDtypeStruct((2, 64, 64), b16)
    pred, grad = pl.pallas_call(
        functools.partial(kernel, groups),
        out_shape=(result, result),
        in_specs=[hbm] * 6,
        out_specs=(vmem, vmem),
        scratch_shapes=[
            pltpu.VMEM((2, 2, 64, 64), b16),
            pltpu.VMEM((2, PANELS, 64, 128), b16),
            pltpu.VMEM((128, 512), b16),
            pltpu.VMEM((128, 512), b16),
            pltpu.VMEM((groups, 2, PANELS, 64, 128), b16),
            pltpu.VMEM((groups, 2, PANELS, 64, 128), b16),
            pltpu.VMEM((groups, 128, 128), b16),
            pltpu.VMEM((groups, 128, 128), b16),
            pltpu.VMEM((groups, 128, 128), b16),
            pltpu.VMEM((groups, 128, 128), b16),
            pltpu.VMEM((512, 128), f32),
            pltpu.VMEM((512, 128), f32),
            pltpu.VMEM((2, PANELS, 64, 128), f32),
            pltpu.VMEM((2, PANELS, 64, 128), b16),
            pltpu.VMEM((2, 3, 64, 128), b16),
            pltpu.SMEM((tiles, tiles), jnp.int32),
            pltpu.SMEM((tiles, tiles), jnp.int32),
            dma((2,)), dma((2,)), dma((2,)),
            dma((3,)), dma((3,)),
            dma((len(V_CHUNKS), 3)), dma((len(V_CHUNKS), 3)),
            dma((len(U_CHUNKS), 3)), dma((len(U_CHUNKS), 3)),
            dma((groups,)), dma((groups,)), dma((groups,)), dma((groups,)),
            dma((2, 3)), dma((2, 3)),
        ],
        compiler_params=pltpu.CompilerParams(
            collective_id=0, has_side_effects=True, vmem_limit_bytes=60 << 20
        ),
        cost_estimate=pl.CostEstimate(flops=1 << 30, bytes_accessed=4 << 20, transcendentals=0),
    )(wavefield, residual, v_local, u_local, tile_ranks, tile_present)
    return pred, grad


def solution(mesh):
    return jax.shard_map(
        on_device,
        mesh=mesh,
        in_specs=(
            P(None, ("tile", "panel"), None),
            P(None, ("tile", "panel"), None),
            P(None, "tile", None, "panel", None),
            P("tile", None, None, "panel", None),
            P(),
            P(),
        ),
        out_specs=(P(None, ("tile", "panel"), None), P(None, ("tile", "panel"), None)),
        check_vma=False,
    )
```

time: 257 us -> 85.7 us (0.33)
  the two profiles are of different devices: /device:TPU:1 before, /device:TPU:152 now
where the time goes in v1:
time: 85.7 us; the launch traced here: 85.4 us
  Pallas kernels  82.1 us (96%)
  local copies, waits for them, and re-layouts  2.75 us (3%)
    pallas_call x1, Pallas kernels, on_device(): pl.pallas_call(functools.partial(kernel, groups), out_shape=(result, resu...  82.1 us
    unnamed x2, local copies, waits for them, and re-layouts  2.75 us

profile of v1, /device:TPU:152, one launch (start us, length us, event | category | flops | bytes accessed | tf_op | source)
XLA Modules:
  0.0 85.4 jit_solution(15155155008492566950)
XLA Ops:
  0.6 82.1 %shard_map.77 = (bf16[2,64,64]{2,1,0:T(8,128)(2,1)}, bf16[2,64,64]{2,1,0:T(8,128)(2,1)}) custom-call(bf16[2,64,64]{2,1,0:T(8,128)(2,1)} %wave_hbm.1, bf16[2,64,64]{2,1,0:T(8,128)(2,1)} %resid_hbm.1, bf16[16,4,2,64,128]{4,3,2,1,0:T(8,128)(2,1)} %bitcast.2, bf16[16,4,2,64,128]{4,3,2,1,0:T(8,128)(2,1)} %bitcast.3, s32[64,64]{1,0:T(8,128)} %rank_hbm.1, ...), custom_call_target="tpu_custom_call" | custom-call | flops 1073741824 | bytes 4194304 | tf_op jit(solution)/shard_map/pallas_call | solution.py:261
  82.7 1.4 %copy.10 = bf16[2,64,64]{2,1,0:T(8,128)(2,1)} copy(bf16[2,64,64]{2,1,0:T(8,128)(2,1)} %get-tuple-element.4) | data formatting | bytes 32768
  84.1 1.4 %copy.11 = bf16[2,64,64]{2,1,0:T(8,128)(2,1)} copy(bf16[2,64,64]{2,1,0:T(8,128)(2,1)} %get-tuple-element.5) | data formatting | bytes 32768

commit v2 on v1

--- a/solution.py
+++ b/solution.py
@@ -9,17 +9,21 @@
 
 MESH = pl.DeviceIdType.MESH
 PANELS = 4
-V_CHUNKS = (4, 4, 4, 4)
-U_CHUNKS = (4, 4, 4, 2, 1, 1)
-
-
-def spans(sizes):
-    starts = []
-    at = 0
-    for size in sizes:
-        starts.append((at, size))
-        at += size
-    return starts
+SIDE = 4
+FAR_FIRST = (2, 1, 3, 0)
+LOOKAHEAD = 4
+
+
+def column(z):
+    return tuple((y, z) for y in FAR_FIRST)
+
+
+V_CHUNKS = tuple(column(z) for z in FAR_FIRST)
+U_CHUNKS = tuple(column(z) for z in FAR_FIRST[:-1]) + tuple((spot,) for spot in column(0))
+
+
+def opposite(chunk):
+    return tuple(((SIDE - y) % SIDE, (SIDE - z) % SIDE) for y, z in chunk)
 
 
 def kernel(
@@ -29,7 +33,7 @@
     raw, joined, vec_w, vec_r, v_all, u_all, f_send, f_recv, a_send, a_recv,
     acc_p, acc_g, own_sum, part_send, part_recv, ranks, present,
     raw_sem, rank_sem, own_sem, x_send, x_recv, v_ssem, v_rsem, u_ssem, u_rsem,
-    f_ssem, f_rsem, a_ssem, a_rsem, p_ssem, p_rsem,
+    f_ssem, f_rsem, a_ssem, a_rsem, p_ssem, p_rsem, stage_sem,
 ):
     t = lax.axis_index("tile")
     p = lax.axis_index("panel")
@@ -37,6 +41,31 @@
     low = t % PANELS
     q = (p + PANELS - low) % PANELS
     alone = q == low
+
+    row, col = me // SIDE, me % SIDE
+
+    def place(spot):
+        return (row + spot[0]) % SIDE, (col + spot[1]) % SIDE
+
+    def slot(spot):
+        y, z = place(spot)
+        return SIDE * y + z
+
+    def view(ref, chunk, *rest):
+        y, z = place(chunk[0])
+        return ref.at[(y if len(chunk) == 1 else slice(None), z) + rest]
+
+    def device_at(y, z, kind):
+        return {"tile": PANELS * (SIDE * y + z) + kind, "panel": p}
+
+    left, above = device_at(0, me - 1, low), device_at(0, me - SIDE, low)
+    right, below = device_at(0, me + 1, low), device_at(0, me + SIDE, low)
+    has_right = col < SIDE - 1
+    has_below = jnp.logical_and(col == 0, row < SIDE - 1)
+    mirror = device_at(row, col, q)
+
+    def signal(sem, device):
+        pl.semaphore_signal(sem, inc=1, device_id=(device["tile"], device["panel"]), device_id_type=MESH)
 
     raw_copies = [
         pltpu.make_async_copy(wave_hbm, raw.at[0], raw_sem.at[0]),
@@ -47,8 +76,8 @@
         pltpu.make_async_copy(present_hbm, present, rank_sem.at[1]),
     ]
     own_copies = [
-        pltpu.make_async_copy(v_hbm.at[:, q], v_all.at[:, :, p], own_sem.at[0]),
-        pltpu.make_async_copy(u_hbm.at[:, q], u_all.at[:, :, p], own_sem.at[1]),
+        pltpu.make_async_copy(v_hbm.at[:, :, q], v_all.at[:, :, :, p], own_sem.at[0]),
+        pltpu.make_async_copy(u_hbm.at[:, :, q], u_all.at[:, :, :, p], own_sem.at[1]),
     ]
     for copy in raw_copies + rank_copies:
         copy.start()
@@ -57,16 +86,20 @@
     for d in (1, 2, 3):
         pl.semaphore_signal(barrier, inc=1, device_id=(t, (p + d) % PANELS), device_id_type=MESH)
 
-    def greet(n, carry):
-        other = PANELS * n + q
-
-        @pl.when(other != t)
+    @pl.when(jnp.logical_not(alone))
+    def _():
+        signal(barrier, mirror)
+
+    def tell_children(sem):
+        @pl.when(has_right)
         def _():
-            pl.semaphore_signal(barrier, inc=1, device_id=(other, p), device_id_type=MESH)
-
-        return carry
-
-    lax.fori_loop(0, groups, greet, 0)
+            signal(sem, right)
+
+        @pl.when(has_below)
+        def _():
+            signal(sem, below)
+
+    tell_children(barrier)
     for copy in own_copies:
         copy.start()
     for copy in raw_copies:
@@ -74,13 +107,7 @@
     for k in (0, 1):
         joined[k, p] = jnp.concatenate([raw[k, 0], raw[k, 1]], axis=1)
 
-    @pl.when(alone)
-    def _():
-        pl.semaphore_wait(barrier, 3 + groups - 1)
-
-    @pl.when(jnp.logical_not(alone))
-    def _():
-        pl.semaphore_wait(barrier, 3 + groups)
+    pl.semaphore_wait(barrier, 3 + (me > 0).astype(jnp.int32) + (q != low).astype(jnp.int32))
 
     def vec_copy(d):
         return pltpu.make_async_remote_copy(
@@ -95,33 +122,64 @@
             device_id=(t, source), device_id_type=MESH,
         )
 
-    def factor_copy(src, dst, ssem, rsem, c, start, size, d):
-        return pltpu.make_async_remote_copy(
-            src.at[pl.ds(start, size), (q + d) % PANELS],
-            dst.at[pl.ds(start, size), :, p],
+    def factor_copy(src, dst, ssem, rsem, c, chunk, d):
+        return pltpu.make_async_remote_copy(
+            view(src, chunk, (q + d) % PANELS),
+            view(dst, chunk, slice(None), p),
             ssem.at[c, d - 1], rsem.at[c, d - 1],
             device_id=(t, (p + d) % PANELS), device_id_type=MESH,
         )
 
-    def factor_arrival(src, dst, ssem, rsem, c, start, size, d):
+    def factor_arrival(src, dst, ssem, rsem, c, chunk, d):
         source = (p + PANELS - d) % PANELS
         return pltpu.make_async_remote_copy(
-            src.at[pl.ds(start, size), q],
-            dst.at[pl.ds(start, size), :, source],
+            view(src, chunk, q),
+            view(dst, chunk, slice(None), source),
             ssem.at[c, d - 1], rsem.at[c, d - 1],
             device_id=(t, source), device_id_type=MESH,
         )
 
     for d in (1, 3, 2):
         vec_copy(d).start()
-    v_spans = spans(V_CHUNKS)
-    u_spans = spans(U_CHUNKS)
-    for c, (start, size) in enumerate(v_spans):
-        for d in (2, 1, 3):
-            factor_copy(v_hbm, v_all, v_ssem, v_rsem, c, start, size, d).start()
-    for c, (start, size) in enumerate(u_spans):
-        for d in (2, 1, 3):
-            factor_copy(u_hbm, u_all, u_ssem, u_rsem, c, start, size, d).start()
+    v_parts = (v_hbm, v_all, v_ssem, v_rsem)
+    u_parts = (u_hbm, u_all, u_ssem, u_rsem)
+    plan = [(v_parts, c, chunk) for c, chunk in enumerate(V_CHUNKS)]
+    plan += [(u_parts, c, chunk) for c, chunk in enumerate(U_CHUNKS)]
+    started = []
+
+    def send_until(last):
+        for parts, c, chunk in plan[len(started) : last]:
+            started.append(c)
+            for d in (2, 1, 3):
+                factor_copy(*parts, c, chunk, d).start()
+
+    send_until(LOOKAHEAD)
+    @pl.when(has_right)
+    def _():
+        pl.semaphore_wait(stage_sem.at[0], 1)
+
+    @pl.when(has_below)
+    def _():
+        pl.semaphore_wait(stage_sem.at[3], 1)
+
+    @pl.when(col > 0)
+    def _():
+        signal(stage_sem.at[0], left)
+
+    @pl.when(jnp.logical_and(col == 0, row > 0))
+    def _():
+        signal(stage_sem.at[3], above)
+
+    @pl.when(me > 0)
+    def _():
+        pl.semaphore_wait(stage_sem.at[1], 1)
+
+    tell_children(stage_sem.at[1])
+
+    @pl.when(jnp.logical_not(alone))
+    def _():
+        signal(stage_sem.at[2], mirror)
+        pl.semaphore_wait(stage_sem.at[2], 1)
 
     acc_p[...] = jnp.zeros_like(acc_p)
     acc_g[...] = jnp.zeros_like(acc_g)
@@ -145,14 +203,13 @@
 
     levels = lax.broadcasted_iota(jnp.int32, (1, 128), 1)
 
-    def project(factor, vec, send, recv, ssem, rsem, start, size, column):
-        for n0 in range(start, start + size, 2):
-            many = min(2, start + size - n0)
-            joint = [factor[n0 + k].reshape(512, 128) for k in range(many)]
-            joint = joint[0] if many == 1 else jnp.concatenate(joint, axis=1)
+    def project(factor, vec, send, recv, ssem, rsem, chunk, column):
+        for at in range(0, len(chunk), 2):
+            slots = [slot(spot) for spot in chunk[at : at + 2]]
+            joint = [factor[place(spot)].reshape(512, 128) for spot in chunk[at : at + 2]]
+            joint = joint[0] if len(slots) == 1 else jnp.concatenate(joint, axis=1)
             space = jnp.dot(vec[...], joint, preferred_element_type=jnp.float32)
-            for k in range(many):
-                n = n0 + k
+            for k, n in enumerate(slots):
                 other = PANELS * n + q
                 if column:
                     rank, here = ranks[other, t], present[other, t]
@@ -170,15 +227,15 @@
                 def _():
                     block_own(send, recv, rsem, n).start()
 
-    def expand(factor, recv, rsem, acc, start, size):
-        for n0 in range(start, start + size, 2):
-            many = min(2, start + size - n0)
-            for k in range(many):
-                block_own(recv, recv, rsem, n0 + k).wait()
-            left = [factor[n0 + k].reshape(512, 128) for k in range(many)]
-            right = [recv[n0 + k] for k in range(many)]
-            left = left[0] if many == 1 else jnp.concatenate(left, axis=1)
-            right = right[0] if many == 1 else jnp.concatenate(right, axis=1)
+    def expand(factor, recv, rsem, acc, chunk):
+        for at in range(0, len(chunk), 2):
+            slots = [slot(spot) for spot in chunk[at : at + 2]]
+            for n in slots:
+                block_own(recv, recv, rsem, n).wait()
+            left = [factor[place(spot)].reshape(512, 128) for spot in chunk[at : at + 2]]
+            right = [recv[n] for n in slots]
+            left = left[0] if len(slots) == 1 else jnp.concatenate(left, axis=1)
+            right = right[0] if len(slots) == 1 else jnp.concatenate(right, axis=1)
             acc[...] += lax.dot_general(
                 left, right, (((1,), (1,)), ((), ())), preferred_element_type=jnp.float32
             )
@@ -210,30 +267,30 @@
         out[1] = total[:, 64:].astype(jnp.bfloat16)
 
     own_copies[0].wait()
-    for c, (start, size) in enumerate(v_spans):
+    for c, chunk in enumerate(V_CHUNKS):
         for d in (1, 3, 2):
-            factor_arrival(v_hbm, v_all, v_ssem, v_rsem, c, start, size, d).wait_recv()
-        project(v_all, vec_w, f_send, f_recv, f_ssem, f_rsem, start, size, True)
+            factor_arrival(*v_parts, c, chunk, d).wait_recv()
+        send_until(c + 1 + LOOKAHEAD)
+        project(v_all, vec_w, f_send, f_recv, f_ssem, f_rsem, chunk, True)
     own_copies[1].wait()
-    for c, (start, size) in enumerate(u_spans):
+    for c, chunk in enumerate(U_CHUNKS):
         for d in (1, 3, 2):
-            factor_arrival(u_hbm, u_all, u_ssem, u_rsem, c, start, size, d).wait_recv()
-        project(u_all, vec_r, a_send, a_recv, a_ssem, a_rsem, start, size, False)
-        expand(u_all, f_recv, f_rsem, acc_p, start, size)
-        if c > 0:
-            expand(v_all, a_recv, a_rsem, acc_g, *u_spans[c - 1])
+            factor_arrival(*u_parts, c, chunk, d).wait_recv()
+        send_until(len(V_CHUNKS) + c + 1 + LOOKAHEAD)
+        project(u_all, vec_r, a_send, a_recv, a_ssem, a_rsem, chunk, False)
+        expand(u_all, f_recv, f_rsem, acc_p, chunk)
     send_parts(0, acc_p)
-    expand(v_all, a_recv, a_rsem, acc_g, *u_spans[-1])
+    expand(v_all, a_recv, a_rsem, acc_g, sum((opposite(chunk) for chunk in U_CHUNKS), ()))
     send_parts(1, acc_g)
     finish(0, pred_ref)
     finish(1, grad_ref)
 
     for d in (1, 2, 3):
         vec_copy(d).wait_send()
-        for c, (start, size) in enumerate(v_spans):
-            factor_copy(v_hbm, v_all, v_ssem, v_rsem, c, start, size, d).wait_send()
-        for c, (start, size) in enumerate(u_spans):
-            factor_copy(u_hbm, u_all, u_ssem, u_rsem, c, start, size, d).wait_send()
+        for c, chunk in enumerate(V_CHUNKS):
+            factor_copy(*v_parts, c, chunk, d).wait_send()
+        for c, chunk in enumerate(U_CHUNKS):
+            factor_copy(*u_parts, c, chunk, d).wait_send()
         for k in (0, 1):
             part_copy(k, d).wait_send()
 
@@ -251,8 +308,8 @@
 def on_device(wavefield, residual, v_factors, u_factors, tile_ranks, tile_present):
     tiles = tile_ranks.shape[0]
     groups = tiles // PANELS
-    v_local = v_factors.reshape(groups, PANELS, 2, 64, 128)
-    u_local = u_factors.reshape(groups, PANELS, 2, 64, 128)
+    v_local = v_factors.reshape(SIDE, SIDE, PANELS, 2, 64, 128)
+    u_local = u_factors.reshape(SIDE, SIDE, PANELS, 2, 64, 128)
     hbm = pl.BlockSpec(memory_space=pl.ANY)
     vmem = pl.BlockSpec(memory_space=pltpu.VMEM)
     b16, f32 = jnp.bfloat16, jnp.float32
@@ -268,8 +325,8 @@
             pltpu.VMEM((2, PANELS, 64, 128), b16),
             pltpu.VMEM((128, 512), b16),
             pltpu.VMEM((128, 512), b16),
-            pltpu.VMEM((groups, 2, PANELS, 64, 128), b16),
-            pltpu.VMEM((groups, 2, PANELS, 64, 128), b16),
+            pltpu.VMEM((SIDE, SIDE, 2, PANELS, 64, 128), b16),
+            pltpu.VMEM((SIDE, SIDE, 2, PANELS, 64, 128), b16),
             pltpu.VMEM((groups, 128, 128), b16),
             pltpu.VMEM((groups, 128, 128), b16),
             pltpu.VMEM((groups, 128, 128), b16),
@@ -287,6 +344,7 @@
             dma((len(U_CHUNKS), 3)), dma((len(U_CHUNKS), 3)),
             dma((groups,)), dma((groups,)), dma((groups,)), dma((groups,)),
             dma((2, 3)), dma((2, 3)),
+            pltpu.SemaphoreType.REGULAR((4,)),
         ],
         compiler_params=pltpu.CompilerParams(
             collective_id=0, has_side_effects=True, vmem_limit_bytes=60 << 20

time: 85.7 us -> 69.1 us (0.81)
  the two profiles are of different devices: /device:TPU:152 before, /device:TPU:1 now
where the time goes in v2:
time: 69.1 us; the launch traced here: 68.8 us
  Pallas kernels  65.4 us (95%)
  local copies, waits for them, and re-layouts  2.75 us (4%)
    pallas_call x1, Pallas kernels, on_device(): pl.pallas_call(functools.partial(kernel, groups), out_shape=(result, resu...  65.4 us
    unnamed x2, local copies, waits for them, and re-layouts  2.75 us

profile of v2, /device:TPU:1, one launch (start us, length us, event | category | flops | bytes accessed | tf_op | source)
XLA Modules:
  0.0 68.8 jit_solution(7621770918150922128)
XLA Ops:
  0.6 65.4 %shard_map.77 = (bf16[2,64,64]{2,1,0:T(8,128)(2,1)}, bf16[2,64,64]{2,1,0:T(8,128)(2,1)}) custom-call(bf16[2,64,64]{2,1,0:T(8,128)(2,1)} %wave_hbm.1, bf16[2,64,64]{2,1,0:T(8,128)(2,1)} %resid_hbm.1, bf16[4,4,4,2,64,128]{5,4,3,2,1,0:T(8,128)(2,1)} %bitcast.2, bf16[4,4,4,2,64,128]{5,4,3,2,1,0:T(8,128)(2,1)} %bitcast.3, s32[64,64]{1,0:T(8,128)} %rank_hbm.1, ...), custom_call_target="tpu_custom_call" | custom-call | flops 1073741824 | bytes 4194304 | tf_op jit(solution)/shard_map/pallas_call | solution.py:318
  66.0 1.4 %copy.10 = bf16[2,64,64]{2,1,0:T(8,128)(2,1)} copy(bf16[2,64,64]{2,1,0:T(8,128)(2,1)} %get-tuple-element.4) | data formatting | bytes 32768
  67.4 1.4 %copy.11 = bf16[2,64,64]{2,1,0:T(8,128)(2,1)} copy(bf16[2,64,64]{2,1,0:T(8,128)(2,1)} %get-tuple-element.5) | data formatting | bytes 32768

commit v3 on v2

--- a/solution.py
+++ b/solution.py
@@ -19,7 +19,36 @@
 
 
 V_CHUNKS = tuple(column(z) for z in FAR_FIRST)
-U_CHUNKS = tuple(column(z) for z in FAR_FIRST[:-1]) + tuple((spot,) for spot in column(0))
+U_CHUNKS = (
+    column(2),
+    ((2, 1), (2, 3), (1, 1), (3, 3)),
+    ((3, 1), (1, 3), (0, 1), (0, 3)),
+    ((2, 0),),
+    ((1, 0),),
+    ((3, 0),),
+    ((0, 0),),
+)
+ADJOINT_AFTER = {}
+
+
+def pieces(chunk):
+    if len(chunk) == SIDE and len({z for _, z in chunk}) == 1:
+        return (chunk,)
+    return tuple((spot,) for spot in chunk)
+
+
+def numbered(chunks):
+    count = 0
+    result = []
+    for chunk in chunks:
+        parts = pieces(chunk)
+        result.append((chunk, tuple((count + k, part) for k, part in enumerate(parts))))
+        count += len(parts)
+    return tuple(result), count
+
+
+V_PLAN, V_COUNT = numbered(V_CHUNKS)
+U_PLAN, U_COUNT = numbered(U_CHUNKS)
 
 
 def opposite(chunk):
@@ -29,7 +58,7 @@
 def kernel(
     groups,
     wave_hbm, resid_hbm, v_hbm, u_hbm, rank_hbm, present_hbm,
-    pred_ref, grad_ref,
+    out_ref,
     raw, joined, vec_w, vec_r, v_all, u_all, f_send, f_recv, a_send, a_recv,
     acc_p, acc_g, own_sum, part_send, part_recv, ranks, present,
     raw_sem, rank_sem, own_sem, x_send, x_recv, v_ssem, v_rsem, u_ssem, u_rsem,
@@ -102,57 +131,57 @@
     tell_children(barrier)
     for copy in own_copies:
         copy.start()
+    pl.semaphore_wait(barrier, 3 + (me > 0).astype(jnp.int32) + (q != low).astype(jnp.int32))
+
+    def vec_copy(d):
+        return pltpu.make_async_remote_copy(
+            joined.at[:, p], joined.at[:, p], x_send.at[d - 1], x_recv.at[d - 1],
+            device_id=(t, (p + d) % PANELS), device_id_type=MESH,
+        )
+
+    def vec_arrival(d):
+        source = (p + PANELS - d) % PANELS
+        return pltpu.make_async_remote_copy(
+            joined.at[:, source], joined.at[:, source], x_send.at[d - 1], x_recv.at[d - 1],
+            device_id=(t, source), device_id_type=MESH,
+        )
+
+    def factor_copy(src, dst, ssem, rsem, c, chunk, d):
+        return pltpu.make_async_remote_copy(
+            view(src, chunk, (q + d) % PANELS),
+            view(dst, chunk, slice(None), p),
+            ssem.at[c, d - 1], rsem.at[c, d - 1],
+            device_id=(t, (p + d) % PANELS), device_id_type=MESH,
+        )
+
+    def factor_arrival(src, dst, ssem, rsem, c, chunk, d):
+        source = (p + PANELS - d) % PANELS
+        return pltpu.make_async_remote_copy(
+            view(src, chunk, q),
+            view(dst, chunk, slice(None), source),
+            ssem.at[c, d - 1], rsem.at[c, d - 1],
+            device_id=(t, source), device_id_type=MESH,
+        )
+
+    v_parts = (v_hbm, v_all, v_ssem, v_rsem)
+    u_parts = (u_hbm, u_all, u_ssem, u_rsem)
+    plan = [(v_parts, parts) for _, parts in V_PLAN] + [(u_parts, parts) for _, parts in U_PLAN]
+    started = []
+
+    def send_until(last):
+        for refs, parts in plan[len(started) : last]:
+            started.append(refs)
+            for c, part in parts:
+                for d in (2, 1, 3):
+                    factor_copy(*refs, c, part, d).start()
+
+    send_until(1)
     for copy in raw_copies:
         copy.wait()
     for k in (0, 1):
         joined[k, p] = jnp.concatenate([raw[k, 0], raw[k, 1]], axis=1)
-
-    pl.semaphore_wait(barrier, 3 + (me > 0).astype(jnp.int32) + (q != low).astype(jnp.int32))
-
-    def vec_copy(d):
-        return pltpu.make_async_remote_copy(
-            joined.at[:, p], joined.at[:, p], x_send.at[d - 1], x_recv.at[d - 1],
-            device_id=(t, (p + d) % PANELS), device_id_type=MESH,
-        )
-
-    def vec_arrival(d):
-        source = (p + PANELS - d) % PANELS
-        return pltpu.make_async_remote_copy(
-            joined.at[:, source], joined.at[:, source], x_send.at[d - 1], x_recv.at[d - 1],
-            device_id=(t, source), device_id_type=MESH,
-        )
-
-    def factor_copy(src, dst, ssem, rsem, c, chunk, d):
-        return pltpu.make_async_remote_copy(
-            view(src, chunk, (q + d) % PANELS),
-            view(dst, chunk, slice(None), p),
-            ssem.at[c, d - 1], rsem.at[c, d - 1],
-            device_id=(t, (p + d) % PANELS), device_id_type=MESH,
-        )
-
-    def factor_arrival(src, dst, ssem, rsem, c, chunk, d):
-        source = (p + PANELS - d) % PANELS
-        return pltpu.make_async_remote_copy(
-            view(src, chunk, q),
-            view(dst, chunk, slice(None), source),
-            ssem.at[c, d - 1], rsem.at[c, d - 1],
-            device_id=(t, source), device_id_type=MESH,
-        )
-
-    for d in (1, 3, 2):
+    for d in (2, 1, 3):
         vec_copy(d).start()
-    v_parts = (v_hbm, v_all, v_ssem, v_rsem)
-    u_parts = (u_hbm, u_all, u_ssem, u_rsem)
-    plan = [(v_parts, c, chunk) for c, chunk in enumerate(V_CHUNKS)]
-    plan += [(u_parts, c, chunk) for c, chunk in enumerate(U_CHUNKS)]
-    started = []
-
-    def send_until(last):
-        for parts, c, chunk in plan[len(started) : last]:
-            started.append(c)
-            for d in (2, 1, 3):
-                factor_copy(*parts, c, chunk, d).start()
-
     send_until(LOOKAHEAD)
     @pl.when(has_right)
     def _():
@@ -174,7 +203,13 @@
     def _():
         pl.semaphore_wait(stage_sem.at[1], 1)
 
-    tell_children(stage_sem.at[1])
+    @pl.when(me == 0)
+    def _():
+        def answer(n, carry):
+            signal(stage_sem.at[1], device_at(0, n, low))
+            return carry
+
+        lax.fori_loop(1, groups, answer, 0)
 
     @pl.when(jnp.logical_not(alone))
     def _():
@@ -257,42 +292,45 @@
         for d in (2, 1, 3):
             part_copy(k, d).start()
 
-    def finish(k, out):
+    def finish(k):
         for d in (1, 3, 2):
             part_copy(k, d).wait_recv()
         total = own_sum[k, p]
         for d in (1, 2, 3):
             total = total + part_recv[k, d - 1].astype(jnp.float32)
-        out[0] = total[:, :64].astype(jnp.bfloat16)
-        out[1] = total[:, 64:].astype(jnp.bfloat16)
+        out_ref[k, 0] = total[:, :64].astype(jnp.bfloat16)
+        out_ref[k, 1] = total[:, 64:].astype(jnp.bfloat16)
+
+    def arrive(refs, parts):
+        for c, part in parts:
+            for d in (1, 3, 2):
+                factor_arrival(*refs, c, part, d).wait_recv()
 
     own_copies[0].wait()
-    for c, chunk in enumerate(V_CHUNKS):
-        for d in (1, 3, 2):
-            factor_arrival(*v_parts, c, chunk, d).wait_recv()
+    for c, (chunk, parts) in enumerate(V_PLAN):
+        arrive(v_parts, parts)
         send_until(c + 1 + LOOKAHEAD)
         project(v_all, vec_w, f_send, f_recv, f_ssem, f_rsem, chunk, True)
     own_copies[1].wait()
-    for c, chunk in enumerate(U_CHUNKS):
-        for d in (1, 3, 2):
-            factor_arrival(*u_parts, c, chunk, d).wait_recv()
-        send_until(len(V_CHUNKS) + c + 1 + LOOKAHEAD)
+    done = []
+    for c, (chunk, parts) in enumerate(U_PLAN):
+        arrive(u_parts, parts)
+        send_until(len(V_PLAN) + c + 1 + LOOKAHEAD)
         project(u_all, vec_r, a_send, a_recv, a_ssem, a_rsem, chunk, False)
         expand(u_all, f_recv, f_rsem, acc_p, chunk)
+        for k in ADJOINT_AFTER.get(c, ()):
+            expand(v_all, a_recv, a_rsem, acc_g, opposite(U_CHUNKS[k]))
+            done.append(k)
     send_parts(0, acc_p)
-    expand(v_all, a_recv, a_rsem, acc_g, sum((opposite(chunk) for chunk in U_CHUNKS), ()))
+    rest = sum((opposite(chunk) for k, chunk in enumerate(U_CHUNKS) if k not in done), ())
+    expand(v_all, a_recv, a_rsem, acc_g, rest)
     send_parts(1, acc_g)
-    finish(0, pred_ref)
-    finish(1, grad_ref)
 
     for d in (1, 2, 3):
         vec_copy(d).wait_send()
-        for c, chunk in enumerate(V_CHUNKS):
-            factor_copy(*v_parts, c, chunk, d).wait_send()
-        for c, chunk in enumerate(U_CHUNKS):
-            factor_copy(*u_parts, c, chunk, d).wait_send()
-        for k in (0, 1):
-            part_copy(k, d).wait_send()
+        for refs, parts in plan:
+            for c, part in parts:
+                factor_copy(*refs, c, part, d).wait_send()
 
     def settle(n, carry):
         @pl.when(PANELS * n + q != t)
@@ -303,6 +341,11 @@
         return carry
 
     lax.fori_loop(0, groups, settle, 0)
+    finish(0)
+    finish(1)
+    for d in (1, 2, 3):
+        for k in (0, 1):
+            part_copy(k, d).wait_send()
 
 
 def on_device(wavefield, residual, v_factors, u_factors, tile_ranks, tile_present):
@@ -314,12 +357,11 @@
     vmem = pl.BlockSpec(memory_space=pltpu.VMEM)
     b16, f32 = jnp.bfloat16, jnp.float32
     dma = pltpu.SemaphoreType.DMA
-    result = jax.ShapeDtypeStruct((2, 64, 64), b16)
-    pred, grad = pl.pallas_call(
+    packed = pl.pallas_call(
         functools.partial(kernel, groups),
-        out_shape=(result, result),
+        out_shape=jax.ShapeDtypeStruct((2, 2, 64, 64), b16),
         in_specs=[hbm] * 6,
-        out_specs=(vmem, vmem),
+        out_specs=vmem,
         scratch_shapes=[
             pltpu.VMEM((2, 2, 64, 64), b16),
             pltpu.VMEM((2, PANELS, 64, 128), b16),
@@ -340,18 +382,18 @@
             pltpu.SMEM((tiles, tiles), jnp.int32),
             dma((2,)), dma((2,)), dma((2,)),
             dma((3,)), dma((3,)),
-            dma((len(V_CHUNKS), 3)), dma((len(V_CHUNKS), 3)),
-            dma((len(U_CHUNKS), 3)), dma((len(U_CHUNKS), 3)),
+            dma((V_COUNT, 3)), dma((V_COUNT, 3)),
+            dma((U_COUNT, 3)), dma((U_COUNT, 3)),
             dma((groups,)), dma((groups,)), dma((groups,)), dma((groups,)),
             dma((2, 3)), dma((2, 3)),
             pltpu.SemaphoreType.REGULAR((4,)),
         ],
         compiler_params=pltpu.CompilerParams(
-            collective_id=0, has_side_effects=True, vmem_limit_bytes=60 << 20
+            collective_id=0, has_side_effects=True, vmem_limit_bytes=32 << 20
         ),
         cost_estimate=pl.CostEstimate(flops=1 << 30, bytes_accessed=4 << 20, transcendentals=0),
-    )(wavefield, residual, v_local, u_local, tile_ranks, tile_present)
-    return pred, grad
+    )(*[pltpu.with_memory_space_constraint(x, pltpu.HBM) for x in (wavefield, residual, v_local, u_local, tile_ranks, tile_present)])
+    return packed[0], packed[1]
 
 
 def solution(mesh):

time: 69.1 us -> 64.4 us (0.932)
  Pallas kernels: 65.4 us -> 63 us
  local copies, waits for them, and re-layouts: 2.75 us -> 0.63 us
    unnamed x2 -> x0, local copies, waits for them, and re-layouts: 2.75 us -> none
    pallas_call x1, Pallas kernels: 65.4 us -> 63 us  [on_device(): pl.pallas_call(functools.partial(kernel, groups), out_shape=jax.ShapeDtyp...]
where the time goes in v3:
time: 64.4 us; the launch traced here: 64.3 us
  Pallas kernels  63 us (98%)
    pallas_call x1, Pallas kernels, on_device(): pl.pallas_call(functools.partial(kernel, groups), out_shape=jax.ShapeDtyp...  63 us

profile of v3, /device:TPU:1, one launch (start us, length us, event | category | flops | bytes accessed | tf_op | source)
XLA Modules:
  0.0 64.3 jit_solution(5267290735005134095)
XLA Ops:
  0.6 63.0 %shard_map.77 = bf16[2,2,64,64]{3,2,1,0:T(8,128)(2,1)S(1)} custom-call(bf16[2,64,64]{2,1,0:T(8,128)(2,1)} %wave_hbm.1, bf16[2,64,64]{2,1,0:T(8,128)(2,1)} %resid_hbm.1, bf16[4,4,4,2,64,128]{5,4,3,2,1,0:T(8,128)(2,1)} %bitcast.6, bf16[4,4,4,2,64,128]{5,4,3,2,1,0:T(8,128)(2,1)} %bitcast.7, s32[64,64]{1,0:T(8,128)} %rank_hbm.1, s32[64,64]{1,0:T(8,128)} %present_hbm.1), custom_call_target="tpu_custom_call" | custom-call | flops 1073741824 | bytes 4194304 | tf_op jit(solution)/shard_map/pallas_call | solution.py:360
  63.6 0.6 slice_bitcast_fusion

commit v4 on v3

--- a/solution.py
+++ b/solution.py
@@ -11,24 +11,21 @@
 PANELS = 4
 SIDE = 4
 FAR_FIRST = (2, 1, 3, 0)
-LOOKAHEAD = 4
+LOOKAHEAD = 6
 
 
 def column(z):
     return tuple((y, z) for y in FAR_FIRST)
 
 
-V_CHUNKS = tuple(column(z) for z in FAR_FIRST)
-U_CHUNKS = (
+FAR_CHUNKS = (
     column(2),
     ((2, 1), (2, 3), (1, 1), (3, 3)),
     ((3, 1), (1, 3), (0, 1), (0, 3)),
-    ((2, 0),),
-    ((1, 0),),
-    ((3, 0),),
-    ((0, 0),),
 )
-ADJOINT_AFTER = {}
+V_CHUNKS = FAR_CHUNKS + (column(0),)
+U_CHUNKS = FAR_CHUNKS + tuple((spot,) for spot in column(0))
+ORDER = ("v", "v", "v", "u", "u", "u", "v", "u", "u", "u", "u")
 
 
 def pieces(chunk):
@@ -69,7 +66,8 @@
     me = t // PANELS
     low = t % PANELS
     q = (p + PANELS - low) % PANELS
-    alone = q == low
+    mine = low // 2 * 2 + 1 - low % 2
+    theirs = q // 2 * 2 + 1 - q % 2
 
     row, col = me // SIDE, me % SIDE
 
@@ -108,14 +106,12 @@
         pltpu.make_async_copy(v_hbm.at[:, :, q], v_all.at[:, :, :, p], own_sem.at[0]),
         pltpu.make_async_copy(u_hbm.at[:, :, q], u_all.at[:, :, :, p], own_sem.at[1]),
     ]
-    for copy in raw_copies + rank_copies:
-        copy.start()
 
     barrier = pltpu.get_barrier_semaphore()
     for d in (1, 2, 3):
         pl.semaphore_signal(barrier, inc=1, device_id=(t, (p + d) % PANELS), device_id_type=MESH)
 
-    @pl.when(jnp.logical_not(alone))
+    @pl.when(mine < theirs)
     def _():
         signal(barrier, mirror)
 
@@ -129,9 +125,9 @@
             signal(sem, below)
 
     tell_children(barrier)
-    for copy in own_copies:
+    for copy in raw_copies + rank_copies + own_copies:
         copy.start()
-    pl.semaphore_wait(barrier, 3 + (me > 0).astype(jnp.int32) + (q != low).astype(jnp.int32))
+    pl.semaphore_wait(barrier, 3 + (me > 0).astype(jnp.int32) + (theirs < mine).astype(jnp.int32))
 
     def vec_copy(d):
         return pltpu.make_async_remote_copy(
@@ -165,7 +161,9 @@
 
     v_parts = (v_hbm, v_all, v_ssem, v_rsem)
     u_parts = (u_hbm, u_all, u_ssem, u_rsem)
-    plan = [(v_parts, parts) for _, parts in V_PLAN] + [(u_parts, parts) for _, parts in U_PLAN]
+    left_to_plan = {"v": list(V_PLAN), "u": list(U_PLAN)}
+    steps = [(kind,) + left_to_plan[kind].pop(0) for kind in ORDER]
+    plan = [(v_parts if kind == "v" else u_parts, parts) for kind, _, parts in steps]
     started = []
 
     def send_until(last):
@@ -211,10 +209,15 @@
 
         lax.fori_loop(1, groups, answer, 0)
 
-    @pl.when(jnp.logical_not(alone))
+    @pl.when(theirs < mine)
     def _():
         signal(stage_sem.at[2], mirror)
         pl.semaphore_wait(stage_sem.at[2], 1)
+
+    @pl.when(mine < theirs)
+    def _():
+        pl.semaphore_wait(stage_sem.at[2], 1)
+        signal(stage_sem.at[2], mirror)
 
     acc_p[...] = jnp.zeros_like(acc_p)
     acc_g[...] = jnp.zeros_like(acc_g)
@@ -306,24 +309,20 @@
             for d in (1, 3, 2):
                 factor_arrival(*refs, c, part, d).wait_recv()
 
-    own_copies[0].wait()
-    for c, (chunk, parts) in enumerate(V_PLAN):
-        arrive(v_parts, parts)
+    for copy in own_copies:
+        copy.wait()
+    for c, (kind, chunk, parts) in enumerate(steps):
+        arrive(plan[c][0], parts)
         send_until(c + 1 + LOOKAHEAD)
-        project(v_all, vec_w, f_send, f_recv, f_ssem, f_rsem, chunk, True)
-    own_copies[1].wait()
-    done = []
-    for c, (chunk, parts) in enumerate(U_PLAN):
-        arrive(u_parts, parts)
-        send_until(len(V_PLAN) + c + 1 + LOOKAHEAD)
-        project(u_all, vec_r, a_send, a_recv, a_ssem, a_rsem, chunk, False)
-        expand(u_all, f_recv, f_rsem, acc_p, chunk)
-        for k in ADJOINT_AFTER.get(c, ()):
-            expand(v_all, a_recv, a_rsem, acc_g, opposite(U_CHUNKS[k]))
-            done.append(k)
+        if kind == "v":
+            project(v_all, vec_w, f_send, f_recv, f_ssem, f_rsem, chunk, True)
+        else:
+            project(u_all, vec_r, a_send, a_recv, a_ssem, a_rsem, chunk, False)
+            if len(chunk) > 1:
+                expand(u_all, f_recv, f_rsem, acc_p, chunk)
+    expand(u_all, f_recv, f_rsem, acc_p, V_CHUNKS[-1])
     send_parts(0, acc_p)
-    rest = sum((opposite(chunk) for k, chunk in enumerate(U_CHUNKS) if k not in done), ())
-    expand(v_all, a_recv, a_rsem, acc_g, rest)
+    expand(v_all, a_recv, a_rsem, acc_g, sum((opposite(chunk) for chunk in U_CHUNKS), ()))
     send_parts(1, acc_g)
 
     for d in (1, 2, 3):

time: 64.4 us -> 64.2 us (level)
  no operation moved by 1% of the time
where the time goes in v4:
time: 64.2 us; the launch traced here: 63.7 us
  Pallas kernels  62.4 us (97%)
    pallas_call x1, Pallas kernels, on_device(): pl.pallas_call(functools.partial(kernel, groups), out_shape=jax.ShapeDtyp...  62.4 us

profile of v4, /device:TPU:1, one launch (start us, length us, event | category | flops | bytes accessed | tf_op | source)
XLA Modules:
  0.0 63.7 jit_solution(614151811995888910)
XLA Ops:
  0.6 62.4 %shard_map.77 = bf16[2,2,64,64]{3,2,1,0:T(8,128)(2,1)S(1)} custom-call(bf16[2,64,64]{2,1,0:T(8,128)(2,1)} %wave_hbm.1, bf16[2,64,64]{2,1,0:T(8,128)(2,1)} %resid_hbm.1, bf16[4,4,4,2,64,128]{5,4,3,2,1,0:T(8,128)(2,1)} %bitcast.6, bf16[4,4,4,2,64,128]{5,4,3,2,1,0:T(8,128)(2,1)} %bitcast.7, s32[64,64]{1,0:T(8,128)} %rank_hbm.1, s32[64,64]{1,0:T(8,128)} %present_hbm.1), custom_call_target="tpu_custom_call" | custom-call | flops 1073741824 | bytes 4194304 | tf_op jit(solution)/shard_map/pallas_call | solution.py:359
  63.1 0.6 slice_bitcast_fusion

commit v5 on v4

--- a/solution.py
+++ b/solution.py
@@ -170,7 +170,7 @@
         for refs, parts in plan[len(started) : last]:
             started.append(refs)
             for c, part in parts:
-                for d in (2, 1, 3):
+                for d in (1, 3, 2):
                     factor_copy(*refs, c, part, d).start()
 
     send_until(1)

time: 64.2 us -> 64.3 us (level)
  no operation moved by 1% of the time
where the time goes in v5:
time: 64.3 us; the launch traced here: 64.2 us
  Pallas kernels  63 us (98%)
    pallas_call x1, Pallas kernels, on_device(): pl.pallas_call(functools.partial(kernel, groups), out_shape=jax.ShapeDtyp...  63 us

profile of v5, /device:TPU:1, one launch (start us, length us, event | category | flops | bytes accessed | tf_op | source)
XLA Modules:
  0.0 64.2 jit_solution(3717699821827286263)
XLA Ops:
  0.6 63.0 %shard_map.77 = bf16[2,2,64,64]{3,2,1,0:T(8,128)(2,1)S(1)} custom-call(bf16[2,64,64]{2,1,0:T(8,128)(2,1)} %wave_hbm.1, bf16[2,64,64]{2,1,0:T(8,128)(2,1)} %resid_hbm.1, bf16[4,4,4,2,64,128]{5,4,3,2,1,0:T(8,128)(2,1)} %bitcast.6, bf16[4,4,4,2,64,128]{5,4,3,2,1,0:T(8,128)(2,1)} %bitcast.7, s32[64,64]{1,0:T(8,128)} %rank_hbm.1, s32[64,64]{1,0:T(8,128)} %present_hbm.1), custom_call_target="tpu_custom_call" | custom-call | flops 1073741824 | bytes 4194304 | tf_op jit(solution)/shard_map/pallas_call | solution.py:359
  63.6 0.6 slice_bitcast_fusion
